TPU v7x, 32 devices: a whole 2x2x4 slice. The times are simulated.
32 devices in a mesh: groups: 1, ep: 32 (over z, y, x, core).
Axes of the slice: x: 2, y: 2, z: 4, core: 2. Of those that a mesh axis runs over, the one named last changes fastest.
Arguments:
- queries: bfloat16 [512, 4096], P(('groups', 'ep')), may hold values from -6 to 6
- keys: bfloat16 [512, 192, 256], P(('groups', 'ep')), may hold values from -6 to 6
- values: bfloat16 [512, 192, 256], P(('groups', 'ep')), may hold values from -6 to 6
- kv_lengths: int32 [512], P(('groups', 'ep')), may hold values from 2 to 192
- residual: bfloat16 [512, 4096], P(('groups', 'ep')), may hold values from -6 to 6
- norm_gain: bfloat16 [4096], replicated, may hold values from 0.5 to 1.5
- routes: int32 [512, 8], P(('groups', 'ep')), may hold values from 0 to 15, all different within a row; in each aligned block of 8 rows (0 to 7, 8 to 15, ...) at most 8 rows name the same one
- route_weights: bfloat16 [512, 8], P(('groups', 'ep')), may hold values from 0.099609375 to 0.5
- gate_weight: bfloat16 [32, 4096, 384], P('ep'), may hold values from -0.09375 to 0.09375
- up_weight: bfloat16 [32, 4096, 384], P('ep'), may hold values from -0.09375 to 0.09375
- down_weight: bfloat16 [32, 384, 4096], P('ep'), may hold values from -0.21875 to 0.21875
Outputs:
- layer_out: bfloat16 [512, 4096], P(('groups', 'ep'))
Inputs may be any that keep to these rules, and one draw needn't show every extreme that they name: `routes`: in each aligned block of 8 rows no expert is named by more than 8 rows.
All inputs are finite; a program needn't handle non-finite values.
Results may differ from a plain program's by a relative error of at most 0.0075.
Values may be sent and summed in bfloat16 or wider, within the bound.
A program may use at most 128 MiB of HBM per device.

v0:
```python
import jax
import jax.numpy as jnp
from jax import lax
from jax.sharding import PartitionSpec as P

KVH = 2
TOP = 8
MBATCH = 2
MB_ROWS = 8


def swapped(shard, axis, bit):
    return lax.ppermute(shard, axis, [(i, i ^ 1 << bit) for i in range(lax.axis_size(axis))])


def attention_rows(query_rows, key_rows, value_rows, length_rows):
    row_count = query_rows.shape[0]
    positions = key_rows.shape[1]
    head_dim = key_rows.shape[2] // KVH
    query_heads = query_rows.reshape(row_count, KVH, -1, head_dim)
    key_heads = key_rows.reshape(row_count, positions, KVH, head_dim)
    value_heads = value_rows.reshape(row_count, positions, KVH, head_dim)
    scores = jnp.einsum(
        "rgqd,rcgd->rgqc", query_heads, key_heads, preferred_element_type=jnp.float32
    ) * head_dim ** (-0.5)
    visible = jnp.arange(positions, dtype=jnp.int32)[None, :] < length_rows[:, None]
    scores = jnp.where(visible[:, None, None, :], scores, -1e30)
    highest = jnp.max(scores, axis=-1, keepdims=True)
    raw_weights = jnp.exp(scores - highest)
    weights = (raw_weights / jnp.sum(raw_weights, axis=-1, keepdims=True)).astype(jnp.bfloat16)
    mixed_heads = jnp.einsum(
        "rgqc,rcgd->rgqd", weights, value_heads, preferred_element_type=jnp.float32
    )
    return mixed_heads.astype(jnp.bfloat16).reshape(row_count, -1)


def slot_tables(route_block, weight_block, experts, capacity):
    expert_ids = jnp.arange(experts, dtype=jnp.int32)
    onehot = (route_block[:, :, None] == expert_ids).astype(jnp.int32)
    chosen = jnp.sum(onehot, axis=1)
    earlier = jnp.cumsum(chosen, axis=0) - chosen
    slot_rank = jnp.sum(onehot * earlier[:, None, :], axis=2)
    target = route_block * capacity + slot_rank
    slot_ids = jnp.arange(experts * capacity, dtype=jnp.int32)
    slot_hits = target[:, :, None] == slot_ids
    select = jnp.sum(slot_hits.astype(jnp.float32), axis=1).astype(jnp.bfloat16)
    weighted = jnp.sum(
        jnp.where(slot_hits, weight_block.astype(jnp.float32)[:, :, None], jnp.float32(0.0)), axis=1
    )
    return (select, weighted.astype(jnp.bfloat16))


def expert_block(rows_in, gate_half, up_half, down_half):
    gate_values = jnp.dot(rows_in, gate_half, preferred_element_type=jnp.float32)
    up_values = jnp.dot(rows_in, up_half, preferred_element_type=jnp.float32)
    hidden = (jax.nn.silu(gate_values) * up_values).astype(jnp.bfloat16)
    return jnp.dot(hidden, down_half, preferred_element_type=jnp.float32)


def local(
    queries,
    keys,
    values,
    kv_lengths,
    residual,
    norm_gain,
    routes,
    route_weights,
    gate_weight,
    up_weight,
    down_weight,
):
    devices = lax.axis_size("ep")
    experts = devices // 2
    model_width = residual.shape[1]
    half_width = model_width // 2
    capacity = min(MB_ROWS, 2 * max(1, MB_ROWS * TOP // experts))
    lower_half = lax.axis_index("ep") % 2 == 0
    gain_values = norm_gain.astype(jnp.float32)
    results = []
    for micro_batch in range(MBATCH):
        first_row = micro_batch * MB_ROWS
        finish = first_row + MB_ROWS
        attended = attention_rows(
            queries[first_row:finish],
            keys[first_row:finish],
            values[first_row:finish],
            kv_lengths[first_row:finish],
        )
        middle = residual[first_row:finish].astype(jnp.float32) + attended.astype(jnp.float32)
        mean_square = jnp.mean(middle * middle, axis=-1, keepdims=True)
        normed = (middle * lax.rsqrt(mean_square + 1e-06) * gain_values).astype(jnp.bfloat16)
        select, weighted = slot_tables(
            routes[first_row:finish], route_weights[first_row:finish], experts, capacity
        )
        outgoing = jnp.dot(select.T, normed, preferred_element_type=jnp.float32).astype(
            jnp.bfloat16
        )
        copies = jnp.broadcast_to(
            outgoing.reshape(experts, 1, capacity, model_width), (experts, 2, capacity, model_width)
        )
        arrived = lax.all_to_all(
            copies.reshape(devices, capacity, model_width),
            "ep",
            split_axis=0,
            concat_axis=0,
            tiled=True,
        )
        partial_out = expert_block(
            arrived.reshape(devices * capacity, model_width),
            gate_weight[0],
            up_weight[0],
            down_weight[0],
        )
        partial_out = partial_out.reshape(devices, capacity, 2, half_width)
        kept_sums = jnp.where(lower_half, partial_out[:, :, 0], partial_out[:, :, 1])
        handed = jnp.where(lower_half, partial_out[:, :, 1], partial_out[:, :, 0])
        partner_sum = swapped(handed, "ep", 0)
        finished = (kept_sums + partner_sum).astype(jnp.bfloat16)
        returned = lax.all_to_all(finished, "ep", split_axis=0, concat_axis=0, tiled=True)
        rebuilt = (
            returned.reshape(experts, 2, capacity, half_width)
            .transpose(0, 2, 1, 3)
            .reshape(experts * capacity, model_width)
        )
        combined = jnp.dot(weighted, rebuilt, preferred_element_type=jnp.float32)
        results.append((middle + combined).astype(jnp.bfloat16))
    return jnp.concatenate(results, axis=0)


def solution(mesh):
    in_specs = (
        P(("groups", "ep"), None),
        P(("groups", "ep"), None, None),
        P(("groups", "ep"), None, None),
        P(("groups", "ep")),
        P(("groups", "ep"), None),
        P(),
        P(("groups", "ep"), None),
        P(("groups", "ep"), None),
        P("ep", None, None),
        P("ep", None, None),
        P("ep", None, None),
    )
    out_specs = P(("groups", "ep"), None)
    return jax.shard_map(local, mesh=mesh, in_specs=in_specs, out_specs=out_specs, check_vma=False)
```

profile of v0, /device:TPU:0, one launch (start us, length us, event | category | flops | bytes accessed | tf_op | source)
XLA Modules:
  0.0 211.0 jit_solution(6133169789124428371)
XLA Ops:
  0.0 0.9 fusion.85
  0.9 1.8 slice_bitcast_fusion.1
  3.3 0.7 copy-done.8
  4.3 1.5 slice_bitcast_fusion
  7.0 1.8 fusion.62
  8.8 1.8 fusion.63
  10.6 0.7 multiply_reduce_fusion.1
  11.8 0.7 fusion.84
  14.9 0.7 convert_element_type.103
  15.6 1.4 select_reduce_fusion.2
  17.0 1.1 fusion.2
  18.1 1.6 broadcast_in_dim.81
  19.7 7.4 %all-to-all-start = ((bf16[32,8,4096]{2,1,0:T(8,128)(2,1)}), bf16[32,8,4096]{2,1,0:T(8,128)(2,1)}, u32[]{:S(2)}, u32[]{:S(2)}) async-start(bf16[32,8,4096]{2,1,0:T(8,128)(2,1)} %bitcast.173), calls=%async_computation | async-start | bytes 4194304 | tf_op jit(solution)/shard_map/all_to_all | solution.py:102
  27.1 1.3 copy.67
  28.5 1.4 convert_reduce_fusion.1
  29.8 1.3 reduce_window_sum.18
  31.1 1.3 sub.35
  32.4 1.3 copy.56
  33.7 1.0 select_reduce_fusion.1
  34.7 0.7 multiply_add_fusion
  35.4 1.4 select_reduce_fusion
  37.3 1.5 fusion.3
  38.8 37.2 %all-to-all-done = bf16[32,8,4096]{2,1,0:T(8,128)(2,1)} async-done(((bf16[32,8,4096]{2,1,0:T(8,128)(2,1)}), bf16[32,8,4096]{2,1,0:T(8,128)(2,1)}, u32[]{:S(2)}, u32[]{:S(2)}) %all-to-all-start) | async-done | bytes 2097184 | tf_op jit(solution)/shard_map/all_to_all | solution.py:102
  76.0 2.9 %broadcast_in_dim.85 = bf16[16,2,8,4096]{3,2,1,0:T(8,128)(2,1)} broadcast(bf16[16,8,4096]{2,1,0:T(8,128)(2,1)} %fusion.3), dimensions={0,2,3} | broadcast | bytes 3145728 | tf_op jit(solution)/shard_map/broadcast_in_dim | solution.py:99
  78.8 4.3 %all-to-all-start.2 = ((bf16[32,8,4096]{2,1,0:T(8,128)(2,1)}), bf16[32,8,4096]{2,1,0:T(8,128)(2,1)}, u32[]{:S(2)}, u32[]{:S(2)}) async-start(bf16[32,8,4096]{2,1,0:T(8,128)(2,1)} %bitcast.172), calls=%async_computation.2 | async-start | bytes 4194304 | tf_op jit(solution)/shard_map/all_to_all | solution.py:102
  83.2 6.1 %dot_general.57 = bf16[2,2048,384]{1,0,2:T(2,128)(2,1)} reshape(bf16[4096,384]{0,1:T(8,128)(2,1)} %bitcast.174) | data formatting | bytes 6291456 | tf_op jit(solution)/shard_map/dot_general | solution.py:57
  89.3 8.7 %copy.48 = bf16[2,2048,384]{2,1,0:T(8,128)(2,1)} copy(bf16[2,2048,384]{1,0,2:T(2,128)(2,1)} %dot_general.57) | data formatting | bytes 6291456 | tf_op jit(solution)/shard_map/dot_general | solution.py:57
  98.1 3.0 %fusion.16 = f32[256,384]{1,0:T(8,128)S(1)} fusion(bf16[1,4096,384]{2,1,0:T(8,128)(2,1)S(1)} %copy-done, bf16[32,8,4096]{2,1,0:T(8,128)(2,1)} %all-to-all-done), kind=kOutput, calls=%fused_computation.20 | convolution fusion | flops 805306368 | bytes 5636096 | tf_op jit(solution)/shard_map/dot_general | solution.py:54
  101.1 3.0 %fusion.52 = bf16[32,8,384,1]{2,1,3,0:T(8,128)(2,1)S(1)} fusion(bf16[1,4096,384]{2,1,0:T(8,128)(2,1)S(1)} %copy-done.15, bf16[32,8,4096]{2,1,0:T(8,128)(2,1)} %all-to-all-done, f32[256,384]{1,0:T(8,128)S(1)} %fusion.16), kind=kOutput, calls=%fused_computation.46 | convolution fusion | flops 805896192 | bytes 5832704 | tf_op jit(solution)/shard_map/dot_general | solution.py:55
  104.2 1.3 fusion.8
  105.5 1.8 select_bitcast_fusion.1
  107.3 0.8 copy-done.3
  108.1 23.8 %all-to-all-done.2 = bf16[32,8,4096]{2,1,0:T(8,128)(2,1)} async-done(((bf16[32,8,4096]{2,1,0:T(8,128)(2,1)}), bf16[32,8,4096]{2,1,0:T(8,128)(2,1)}, u32[]{:S(2)}, u32[]{:S(2)}) %all-to-all-start.2) | async-done | bytes 2097184 | tf_op jit(solution)/shard_map/all_to_all | solution.py:102
  131.9 3.0 %fusion.14 = f32[256,384]{1,0:T(8,128)S(1)} fusion(bf16[1,4096,384]{2,1,0:T(8,128)(2,1)S(1)} %copy-done, bf16[32,8,4096]{2,1,0:T(8,128)(2,1)} %all-to-all-done.2), kind=kOutput, calls=%fused_computation.18 | convolution fusion | flops 805306368 | bytes 5636096 | tf_op jit(solution)/shard_map/dot_general | solution.py:54
  135.0 3.0 %fusion.57 = bf16[32,8,384,1]{2,1,0,3:T(8,128)(2,1)S(1)} fusion(bf16[1,4096,384]{2,1,0:T(8,128)(2,1)S(1)} %copy-done.16, bf16[32,8,4096]{2,1,0:T(8,128)(2,1)} %all-to-all-done.2, f32[256,384]{1,0:T(8,128)S(1)} %fusion.14), kind=kOutput, calls=%fused_computation.47 | convolution fusion | flops 805896192 | bytes 5832704 | tf_op jit(solution)/shard_map/dot_general | solution.py:55
  138.0 2.2 %fusion.6 = f32[32,8,2,2048]{3,1,0,2:T(8,128)S(1)} fusion(bf16[32,8,384,1]{2,1,0,3:T(8,128)(2,1)S(1)} %fusion.57, bf16[2,2048,384,1]{1,0,2,3:T(2,128)(2,1)S(1)} %bitcast.171), kind=kOutput, calls=%fused_computation.10 | convolution fusion | flops 805306368 | bytes 7536640 | tf_op jit(solution)/shard_map/dot_general | solution.py:57
  140.3 1.6 select_bitcast_fusion
  141.9 1.5 copy-done.1
  143.4 1.3 copy-done.4
  144.7 3.0 %fusion.20 = bf16[32,8,2048]{2,1,0:T(8,128)(2,1)} fusion(f32[32,8,2048]{2,1,0:T(8,128)} %collective-permute-done, f32[32,8,2,2048]{3,1,2,0:T(8,128)S(1)} %copy-done.4, pred[]{:T(512)S(6)} %eq.63), kind=kLoop, calls=%fused_computation.25 | loop fusion | flops 1572864 | bytes 7340033 | tf_op jit(solution)/shard_map/convert_element_type | solution.py:119
  147.7 4.1 %all-to-all-start.1 = ((bf16[32,8,2048]{2,1,0:T(8,128)(2,1)}), bf16[32,8,2048]{2,1,0:T(8,128)(2,1)}, u32[]{:S(2)}, u32[]{:S(2)}) async-start(bf16[32,8,2048]{2,1,0:T(8,128)(2,1)} %fusion.20), calls=%async_computation.1 | async-start | bytes 2097152 | tf_op jit(solution)/shard_map/all_to_all | solution.py:120
  151.8 4.3 %fusion.21 = bf16[32,8,2048]{2,1,0:T(8,128)(2,1)} fusion(f32[32,8,2048]{2,1,0:T(8,128)} %collective-permute-done.1, f32[32,8,2,2048]{3,1,0,2:T(8,128)} %copy-done.1, pred[]{:T(512)S(6)} %eq.63), kind=kLoop, calls=%fused_computation.27 | loop fusion | flops 1572864 | bytes 7340033 | tf_op jit(solution)/shard_map/convert_element_type | solution.py:119
  156.1 21.9 %all-to-all-done.1 = bf16[32,8,2048]{2,1,0:T(8,128)(2,1)} async-done(((bf16[32,8,2048]{2,1,0:T(8,128)(2,1)}), bf16[32,8,2048]{2,1,0:T(8,128)(2,1)}, u32[]{:S(2)}, u32[]{:S(2)}) %all-to-all-start.1) | async-done | bytes 1048608 | tf_op jit(solution)/shard_map/all_to_all | solution.py:120
  178.0 3.7 %all-to-all-start.3 = ((bf16[32,8,2048]{2,1,0:T(8,128)(2,1)}), bf16[32,8,2048]{2,1,0:T(8,128)(2,1)}, u32[]{:S(2)}, u32[]{:S(2)}) async-start(bf16[32,8,2048]{2,1,0:T(8,128)(2,1)} %fusion.21), calls=%async_computation.3 | async-start | bytes 2097152 | tf_op jit(solution)/shard_map/all_to_all | solution.py:120
  181.8 2.1 fusion.4
  183.9 24.1 %all-to-all-done.3 = bf16[32,8,2048]{2,1,0:T(8,128)(2,1)} async-done(((bf16[32,8,2048]{2,1,0:T(8,128)(2,1)}), bf16[32,8,2048]{2,1,0:T(8,128)(2,1)}, u32[]{:S(2)}, u32[]{:S(2)}) %all-to-all-start.3) | async-done | bytes 1048608 | tf_op jit(solution)/shard_map/all_to_all | solution.py:120
  208.0 1.5 fusion.5
  209.5 1.5 pad_maximum_fusion
  (52 shorter events, 5.6 us)
Async XLA Ops:
  0.0 98.1 %copy-start = (bf16[1,4096,384]{2,1,0:T(8,128)(2,1)S(1)}, bf16[1,4096,384]{2,1,0:T(8,128)(2,1)}, u32[]{:S(2)}) copy-start(bf16[1,4096,384]{2,1,0:T(8,128)(2,1)} %param.19) | copy-start | bytes 9437188
  0.0 2.7 %copy-start.10 = (bf16[16,4096]{1,0:T(8,128)(2,1)S(1)}, bf16[16,4096]{1,0:T(8,128)(2,1)}, u32[]{:S(2)}) copy-start(bf16[16,4096]{1,0:T(8,128)(2,1)} %param.11) | copy-start | bytes 393220
  0.9 3.4 %copy-start.6 = (bf16[16,192,256]{2,1,0:T(8,128)(2,1)S(1)}, bf16[16,192,256]{2,1,0:T(8,128)(2,1)}, u32[]{:S(2)}) copy-start(bf16[16,192,256]{2,1,0:T(8,128)(2,1)} %param.13) | copy-start | bytes 4718596
  3.3 0.7 copy-start.8
  6.3 0.7 copy-start.9
  6.3 4.3 %copy-start.7 = (bf16[16,4096]{1,0:T(8,128)(2,1)S(1)}, bf16[16,4096]{1,0:T(8,128)(2,1)}, u32[]{:S(2)}) copy-start(bf16[16,4096]{1,0:T(8,128)(2,1)} %param.15) | copy-start | bytes 393220
  7.0 4.8 %copy-start.11 = (s32[16,8]{0,1:T(8,128)S(1)}, s32[16,8]{0,1:T(8,128)}, u32[]{:S(2)}) copy-start(s32[16,8]{0,1:T(8,128)} %param.17) | copy-start | bytes 1540
  7.0 6.6 %copy-start.14 = (bf16[16,8]{0,1:T(8,128)(2,1)S(1)}, bf16[16,8]{0,1:T(8,128)(2,1)}, u32[]{:S(2)}) copy-start(bf16[16,8]{0,1:T(8,128)(2,1)} %param.18) | copy-start | bytes 772
  19.7 56.3 %all-to-all-start = ((bf16[32,8,4096]{2,1,0:T(8,128)(2,1)}), bf16[32,8,4096]{2,1,0:T(8,128)(2,1)}, u32[]{:S(2)}, u32[]{:S(2)}) async-start(bf16[32,8,4096]{2,1,0:T(8,128)(2,1)} %bitcast.173), calls=%async_computation | async-start | bytes 4194304 | tf_op jit(solution)/shard_map/all_to_all | solution.py:102
  78.8 53.1 %all-to-all-start.2 = ((bf16[32,8,4096]{2,1,0:T(8,128)(2,1)}), bf16[32,8,4096]{2,1,0:T(8,128)(2,1)}, u32[]{:S(2)}, u32[]{:S(2)}) async-start(bf16[32,8,4096]{2,1,0:T(8,128)(2,1)} %bitcast.172), calls=%async_computation.2 | async-start | bytes 4194304 | tf_op jit(solution)/shard_map/all_to_all | solution.py:102
  98.1 3.0 %copy-start.15 = (bf16[1,4096,384]{2,1,0:T(8,128)(2,1)S(1)}, bf16[1,4096,384]{2,1,0:T(8,128)(2,1)}, u32[]{:S(2)}) copy-start(bf16[1,4096,384]{2,1,0:T(8,128)(2,1)} %param.20) | copy-start | bytes 9437188
  101.1 3.1 %copy-start.5 = (bf16[2,2048,384]{2,1,0:T(8,128)(2,1)S(1)}, bf16[2,2048,384]{2,1,0:T(8,128)(2,1)}, u32[]{:S(2)}) copy-start(bf16[2,2048,384]{2,1,0:T(8,128)(2,1)} %copy.48) | copy-start | bytes 9437188
  105.5 2.6 %copy-start.3 = (f32[32,8,2,2048]{3,1,2,0:T(8,128)}, f32[32,8,2,2048]{3,1,2,0:T(8,128)S(1)}, u32[]{:S(2)}) copy-start(f32[32,8,2,2048]{3,1,2,0:T(8,128)S(1)} %fusion.8) | copy-start | bytes 12582916
  108.1 35.3 %collective-permute-start = (f32[32,8,2048]{2,1,0:T(8,128)}, f32[32,8,2048]{2,1,0:T(8,128)}, u32[]{:S(2)}, u32[]{:S(2)}) collective-permute-start(f32[32,8,2048]{2,1,0:T(8,128)} %select_bitcast_fusion.1), channel_id=1, source_target_pairs={{0,1},{1,0},{2,3},{3,2},{4,5},{5,4},{6,7},{7,6},{8,9},{9,8},{10,11... | collective-permute-start | bytes 6291464 | tf_op jit(solution)/shard_map/ppermute | solution.py:13
  131.9 3.0 %copy-start.16 = (bf16[1,4096,384]{2,1,0:T(8,128)(2,1)S(1)}, bf16[1,4096,384]{2,1,0:T(8,128)(2,1)}, u32[]{:S(2)}) copy-start(bf16[1,4096,384]{2,1,0:T(8,128)(2,1)} %param.20) | copy-start | bytes 9437188
  135.0 3.1 %copy-start.2 = (bf16[2,2048,384]{1,0,2:T(2,128)(2,1)S(1)}, bf16[2,2048,384]{1,0,2:T(2,128)(2,1)}, u32[]{:S(2)}) copy-start(bf16[2,2048,384]{1,0,2:T(2,128)(2,1)} %dot_general.57) | copy-start | bytes 9437188
  140.3 3.1 %copy-start.1 = (f32[32,8,2,2048]{3,1,0,2:T(8,128)}, f32[32,8,2,2048]{3,1,0,2:T(8,128)S(1)}, u32[]{:S(2)}) copy-start(f32[32,8,2,2048]{3,1,0,2:T(8,128)S(1)} %fusion.6) | copy-start | bytes 12582916
  140.3 4.4 %copy-start.4 = (f32[32,8,2,2048]{3,1,2,0:T(8,128)S(1)}, f32[32,8,2,2048]{3,1,2,0:T(8,128)}, u32[]{:S(2)}) copy-start(f32[32,8,2,2048]{3,1,2,0:T(8,128)} %copy-done.3) | copy-start | bytes 12582916
  143.4 8.4 %collective-permute-start.1 = (f32[32,8,2048]{2,1,0:T(8,128)}, f32[32,8,2048]{2,1,0:T(8,128)}, u32[]{:S(2)}, u32[]{:S(2)}) collective-permute-start(f32[32,8,2048]{2,1,0:T(8,128)} %select_bitcast_fusion), channel_id=1, source_target_pairs={{0,1},{1,0},{2,3},{3,2},{4,5},{5,4},{6,7},{7,6},{8,9},{9,8},{10,11... | collective-permute-start | bytes 6291464 | tf_op jit(solution)/shard_map/ppermute | solution.py:13
  147.7 30.3 %all-to-all-start.1 = ((bf16[32,8,2048]{2,1,0:T(8,128)(2,1)}), bf16[32,8,2048]{2,1,0:T(8,128)(2,1)}, u32[]{:S(2)}, u32[]{:S(2)}) async-start(bf16[32,8,2048]{2,1,0:T(8,128)(2,1)} %fusion.20), calls=%async_computation.1 | async-start | bytes 2097152 | tf_op jit(solution)/shard_map/all_to_all | solution.py:120
  156.1 25.7 %copy-start.12 = (bf16[8,128]{1,0:T(8,128)(2,1)S(1)}, bf16[8,128]{1,0:T(8,128)(2,1)}, u32[]{:S(2)}) copy-start(bf16[8,128]{1,0:T(8,128)(2,1)} %get-tuple-element.7) | copy-start | bytes 6148
  156.1 51.9 %copy-start.13 = (bf16[8,128]{1,0:T(8,128)(2,1)S(1)}, bf16[8,128]{1,0:T(8,128)(2,1)}, u32[]{:S(2)}) copy-start(bf16[8,128]{1,0:T(8,128)(2,1)} %get-tuple-element.9) | copy-start | bytes 6148
  178.0 30.0 %all-to-all-start.3 = ((bf16[32,8,2048]{2,1,0:T(8,128)(2,1)}), bf16[32,8,2048]{2,1,0:T(8,128)(2,1)}, u32[]{:S(2)}, u32[]{:S(2)}) async-start(bf16[32,8,2048]{2,1,0:T(8,128)(2,1)} %fusion.21), calls=%async_computation.3 | async-start | bytes 2097152 | tf_op jit(solution)/shard_map/all_to_all | solution.py:120
where the time goes:
time: 212 us; the launch traced here: 211 us
  waiting for transfers between devices  107 us (50%)
  local copies, waits for them, and re-layouts  32.4 us (15%)
  matrix products  26.4 us (12%)
  other arithmetic  25.2 us (12%)
  starting transfers between devices  19.6 us (9%)
    all_to_all x2, waiting for transfers between devices, local(): lax.all_to_all(copies.reshape(devices, capacity, model_width), 'ep', spli...  61 us
    all_to_all x2, waiting for transfers between devices, local(): lax.all_to_all(finished, 'ep', split_axis=0, concat_axis=0, tiled=True)  46 us
    dot_general x2, local copies, waits for them, and re-layouts, expert_block(): return jnp.dot(hidden, down_half, preferred_element_type=jnp.float32)  14.9 us
    all_to_all x2, starting transfers between devices, local(): lax.all_to_all(copies.reshape(devices, capacity, model_width), 'ep', spli...  11.7 us
    unnamed x41, local copies, waits for them, and re-layouts  9.52 us
    all_to_all x2, starting transfers between devices, local(): lax.all_to_all(finished, 'ep', split_axis=0, concat_axis=0, tiled=True)  7.83 us
    convert_element_type x2, other arithmetic, local(): finished = (kept_sums + partner_sum).astype(jnp.bfloat16)  7.3 us
    dot_general x2, matrix products, expert_block(): up_values = jnp.dot(rows_in, up_half, preferred_element_type=jnp.float32)  6.09 us
  transfers between devices with their start and end apart: 6, of which 4 were waited for; matrix products, arithmetic and copies ran while one was open for 26% of the time, Pallas kernels for 0%

commit v1 on v0

v1 whole, which is shorter than its diff:
```python
import jax
import jax.numpy as jnp
from jax import lax
from jax.sharding import PartitionSpec as P

KVH = 2


def attention_rows(query_rows, key_rows, value_rows, length_rows):
    row_count = query_rows.shape[0]
    positions = key_rows.shape[1]
    head_dim = key_rows.shape[2] // KVH
    query_heads = query_rows.reshape(row_count, KVH, -1, head_dim)
    key_heads = key_rows.reshape(row_count, positions, KVH, head_dim)
    value_heads = value_rows.reshape(row_count, positions, KVH, head_dim)
    scores = jnp.einsum(
        "rgqd,rcgd->rgqc", query_heads, key_heads, preferred_element_type=jnp.float32
    ) * head_dim ** (-0.5)
    visible = jnp.arange(positions, dtype=jnp.int32)[None, :] < length_rows[:, None]
    scores = jnp.where(visible[:, None, None, :], scores, -1e30)
    highest = jnp.max(scores, axis=-1, keepdims=True)
    raw_weights = jnp.exp(scores - highest)
    weights = (raw_weights / jnp.sum(raw_weights, axis=-1, keepdims=True)).astype(jnp.bfloat16)
    mixed_heads = jnp.einsum(
        "rgqc,rcgd->rgqd", weights, value_heads, preferred_element_type=jnp.float32
    )
    return mixed_heads.astype(jnp.bfloat16).reshape(row_count, -1)


def local(
    queries,
    keys,
    values,
    kv_lengths,
    residual,
    norm_gain,
    routes,
    route_weights,
    gate_weight,
    up_weight,
    down_weight,
):
    devices = lax.axis_size("ep")
    experts = devices // 2
    width = residual.shape[1]
    lanes = -(-experts // 128) * 128
    mine = lax.axis_index("ep") // 2
    attended = attention_rows(queries, keys, values, kv_lengths)
    middle = residual.astype(jnp.float32) + attended.astype(jnp.float32)
    mean_square = jnp.mean(middle * middle, axis=-1, keepdims=True)
    normed = (middle * lax.rsqrt(mean_square + 1e-06) * norm_gain.astype(jnp.float32)).astype(
        jnp.bfloat16
    )
    hits = routes[:, :, None] == jnp.arange(lanes, dtype=jnp.int32)
    dense = jnp.sum(
        jnp.where(hits, route_weights.astype(jnp.float32)[:, :, None], 0.0), axis=1
    ).astype(jnp.bfloat16)
    packed = jnp.concatenate([normed, dense], axis=1)
    gathered = lax.all_gather(packed, "ep", axis=0, tiled=True)
    rows = gathered[:, :width]
    scale = jnp.sum(
        jnp.where(
            jnp.arange(lanes, dtype=jnp.int32)[None, :] == mine,
            gathered[:, width:].astype(jnp.float32),
            0.0,
        ),
        axis=1,
        keepdims=True,
    )
    gate_values = jnp.dot(rows, gate_weight[0], preferred_element_type=jnp.float32)
    up_values = jnp.dot(rows, up_weight[0], preferred_element_type=jnp.float32)
    hidden = (jax.nn.silu(gate_values) * up_values).astype(jnp.bfloat16)
    partial_out = jnp.dot(hidden, down_weight[0], preferred_element_type=jnp.float32)
    partial_out = (partial_out * scale).astype(jnp.bfloat16)
    combined = lax.psum_scatter(partial_out, "ep", scatter_dimension=0, tiled=True)
    return (middle + combined.astype(jnp.float32)).astype(jnp.bfloat16)


def solution(mesh):
    rows = P(("groups", "ep"), None)
    cache = P(("groups", "ep"), None, None)
    expert = P("ep", None, None)
    in_specs = (rows, cache, cache, P(("groups", "ep")), rows, P(), rows, rows, expert, expert, expert)
    return jax.shard_map(local, mesh=mesh, in_specs=in_specs, out_specs=rows, check_vma=False)
```

time: 212 us -> 252 us (1.19)
  waiting for transfers between devices: 107 us -> 205 us
  local copies, waits for them, and re-layouts: 32.4 us -> 4.51 us
  starting transfers between devices: 19.6 us -> 0.04 us
  other arithmetic: 25.2 us -> 7.12 us
  between operations: 0.26 us -> 13.4 us
  matrix products: 26.4 us -> 21.2 us
    reduce_scatter x0 -> x1, waiting for transfers between devices: none -> 139 us  [local(): lax.psum_scatter(partial_out, 'ep', scatter_dimension=0, tiled=True)]
    all_to_all x4 -> x0, waiting for transfers between devices: 107 us -> none  [the longest x2 61 us: local(): lax.all_to_all(copies.reshape(devices, capacity, model_width), 'ep', spli...]
    all_gather x0 -> x1, waiting for transfers between devices: none -> 65.3 us  [local(): gathered = lax.all_gather(packed, 'ep', axis=0, tiled=True)]
    all_to_all x4 -> x0, starting transfers between devices: 19.6 us -> none  [the longest x2 11.7 us: local(): lax.all_to_all(copies.reshape(devices, capacity, model_width), 'ep', spli...]
    dot_general x2 -> x0, local copies, waits for them, and re-layouts: 14.9 us -> none  [expert_block(): return jnp.dot(hidden, down_half, preferred_element_type=jnp.float32)]
    unnamed x41 -> x8, local copies, waits for them, and re-layouts: 9.52 us -> 3.17 us
    convert_element_type x4 -> x3, other arithmetic: 8.66 us -> 2.58 us  [the longest x1 1.72 us: local(): return (middle + combined.astype(jnp.float32)).astype(jnp.bfloat16)]
    dot_general x10 -> x2, matrix products: 21.8 us -> 16.2 us  [the longest x1 9.78 us: local(): jnp.dot(hidden, down_weight[0], preferred_element_type=jnp.float32)]
  transfers between devices with their start and end apart: 6 -> 2, of which waited for: 4 -> 2; matrix products, arithmetic and copies ran while one was open for 26% -> 0% of each run, Pallas kernels for 0% -> 0%
where the time goes in v1:
time: 252 us; the launch traced here: 251 us
  waiting for transfers between devices  205 us (81%)
  matrix products  21.2 us (8%)
  between operations  13.4 us (5%)
  other arithmetic  7.12 us (3%)
  local copies, waits for them, and re-layouts  4.51 us (2%)
    reduce_scatter x1, waiting for transfers between devices, local(): lax.psum_scatter(partial_out, 'ep', scatter_dimension=0, tiled=True)  139 us
    all_gather x1, waiting for transfers between devices, local(): gathered = lax.all_gather(packed, 'ep', axis=0, tiled=True)  65.3 us
    dot_general x1, matrix products, local(): jnp.dot(hidden, down_weight[0], preferred_element_type=jnp.float32)  9.78 us
    dot_general x1, matrix products, local(): jnp.dot(rows, gate_weight[0], preferred_element_type=jnp.float32)  6.43 us
  transfers between devices with their start and end apart: 2, of which 2 were waited for; matrix products, arithmetic and copies ran while one was open for 0% of the time, Pallas kernels for 0%

profile of v1, /device:TPU:0, one launch (start us, length us, event | category | flops | bytes accessed | tf_op | source)
XLA Modules:
  0.0 251.2 jit_solution(2514639186090839983)
XLA Ops:
  6.5 0.0 copy-start
  6.5 0.0 all-gather.2.cloned.1.call-start
  6.5 0.9 iota_compare_fusion.1
  7.4 1.4 copy.18
  8.8 1.3 copy.19
  10.2 0.7 convert_element_type.47
  10.9 0.9 copy.22
  11.8 0.0 copy-start.2
  11.8 2.4 fusion.29
  14.2 0.0 copy-start.1
  14.2 0.8 copy-done.1
  15.0 0.9 fusion.46
  15.9 2.7 %fusion.35 = f32[16,2,16,128]{3,2,1,0:T(8,128)S(1)} fusion(f32[16,2,16]{2,1,0:T(2,128)} %fusion.46, f32[16,2,16,192]{3,2,1,0:T(8,128)} %copy-done.1, bf16[16,192,256]{2,1,0:T(8,128)(2,1)} %param.13), kind=kOutput, calls=%fused_computation.22 | convolution fusion | flops 25592512 | bytes 2230272 | tf_op jit(solution)/shard_map/rgqc,rcgd->rgqd/dot_general | solution.py:24
  18.5 0.0 copy-done.2
  18.5 0.3 multiply_reduce_fusion
  18.8 0.8 select_reduce_fusion.1
  19.7 0.2 multiply_convert_fusion.1
  19.8 0.7 pad_maximum_fusion
  20.5 0.0 all-gather.2.cloned.1.call-update
  20.5 0.0 reduce-scatter.2.cloned.1.call-start
  20.6 65.3 %all-gather.2.cloned.1.call-done = bf16[512,4224]{1,0:T(8,128)(2,1)} async-done(((bf16[16,4224]{1,0:T(8,128)(2,1)}), bf16[512,4224]{1,0:T(8,128)(2,1)}) %all-gather.2.cloned.1.call-update) | async-done | bytes 4325392 | tf_op jit(solution)/shard_map/all_gather | solution.py:59
  85.9 1.0 select_reduce_fusion
  86.9 6.4 %fusion.3 = f32[512,384]{1,0:T(8,128)} fusion(bf16[512,4224]{1,0:T(8,128)(2,1)} %all-gather.2.cloned.1.call-done, bf16[1,4096,384]{2,1,0:T(8,128)(2,1)} %param.19), kind=kOutput, calls=%fused_computation.4 | convolution fusion | flops 1610612736 | bytes 8126464 | tf_op jit(solution)/shard_map/dot_general | solution.py:70
  93.4 0.0 copy-done
  93.4 9.8 %multiply_convert_fusion = bf16[512,4096]{1,0:T(8,128)(2,1)} fusion(f32[512]{0:T(512)S(1)} %select_reduce_fusion, bf16[1,384,4096]{2,1,0:T(8,128)(2,1)S(1)} %copy-done, bf16[1,4096,384]{2,1,0:T(8,128)(2,1)} %param.20, bf16[512,4224]{1,0:T(8,128)(2,1)} %all-gather.2.cloned.1.call-done, f32[512,384]{1,0:T(8,128)} %fusion.3), kind=kOutput, calls=%fused_computation.1 | convolution fusion | flops 3226599424 | bytes 15468544 | tf_op jit(solution)/shard_map/dot_general | solution.py:73
  103.1 0.0 reduce-scatter.2.cloned.1.call-update
  103.2 139.4 %reduce-scatter.2.cloned.1.call-done = bf16[16,4096]{1,0:T(8,128)(2,1)} async-done(((bf16[512,4096]{1,0:T(8,128)(2,1)}), bf16[16,4096]{1,0:T(8,128)(2,1)}) %reduce-scatter.2.cloned.1.call-update) | async-done | bytes 131088 | tf_op jit(solution)/shard_map/reduce_scatter | solution.py:75
  242.6 1.7 add_convert_fusion
  (2 shorter events, 0.0 us)
Async XLA Ops:
  6.5 86.8 %copy-start = (bf16[1,384,4096]{2,1,0:T(8,128)(2,1)S(1)}, bf16[1,384,4096]{2,1,0:T(8,128)(2,1)}, u32[]{:S(2)}) copy-start(bf16[1,384,4096]{2,1,0:T(8,128)(2,1)} %param.21) | copy-start | bytes 9437188
  6.5 79.4 %all-gather.2.cloned.1.call-start = ((), (), s32[]{:S(2)}) async-start(), calls=%async_computation.1 | async-start | bytes 4460544 | tf_op jit(solution)/shard_map/all_gather | solution.py:59
  11.8 6.7 %copy-start.2 = (bf16[16,4096]{1,0:T(8,128)(2,1)S(1)}, bf16[16,4096]{1,0:T(8,128)(2,1)}, u32[]{:S(2)}) copy-start(bf16[16,4096]{1,0:T(8,128)(2,1)} %param.15) | copy-start | bytes 393220
  14.2 0.8 copy-start.1
  20.5 222.1 %reduce-scatter.2.cloned.1.call-start = ((), (), s32[]{:S(2)}) async-start(), calls=%async_computation.2 | async-start | bytes 4325376 | tf_op jit(solution)/shard_map/reduce_scatter | solution.py:75
Sparse Core Ops, SparseCore 0:
  20.6 65.2 all-gather.1
  103.3 139.2 reduce-scatter.1

commit v2 on v1

--- a/solution.py
+++ b/solution.py
@@ -1,9 +1,185 @@
+import functools
+
 import jax
 import jax.numpy as jnp
 from jax import lax
+from jax.experimental import pallas as pl
+from jax.experimental.pallas import tpu as pltpu
 from jax.sharding import PartitionSpec as P
 
 KVH = 2
+VMEM_BUDGET = 40 << 20
+
+
+def place(position, devices):
+    quarter, rest = divmod(position, devices // 4)
+    return (0, 2, 1, 3)[quarter] * (devices // 4) + rest
+
+
+def exchange_kernel(
+    devices, own_ref, gate_hbm, up_hbm, down_hbm, out_ref,
+    rows, parts, landed, hidden, gate, up, down,
+    load_sem, gather_send, gather_recv, reduce_send, reduce_recv,
+):
+    stages = devices.bit_length() - 1
+    count, width = own_ref.shape[0], gate_hbm.shape[1]
+    quarter = devices // 4
+    me = lax.axis_index("ep")
+    core = me % 2
+    bits = [1 << b for b in range(stages - 1, 2, -1)] + [4 - 2 * core, 2 + 2 * core, 1]
+    partners = [me + bit * (1 - 2 * ((me // bit) % 2)) for bit in bits]
+
+    loads = [
+        pltpu.make_async_copy(source.at[0], target, load_sem.at[i])
+        for i, (source, target) in enumerate(((gate_hbm, gate), (up_hbm, up), (down_hbm, down)))
+    ]
+    for load in loads:
+        load.start()
+    rows[0] = own_ref[...]
+    barrier = pltpu.get_barrier_semaphore()
+    for partner in partners:
+        pl.semaphore_signal(
+            barrier, inc=1, device_id={"ep": partner}, device_id_type=pl.DeviceIdType.MESH
+        )
+    pl.semaphore_wait(barrier, stages)
+
+    def gather(stage, position):
+        index = (1 << stage) - 1 + position
+        return pltpu.make_async_remote_copy(
+            src_ref=rows.at[place(position, devices)],
+            dst_ref=rows.at[place(position + (1 << stage), devices)],
+            send_sem=gather_send.at[index],
+            recv_sem=gather_recv.at[index],
+            device_id={"ep": partners[stage]},
+            device_id_type=pl.DeviceIdType.MESH,
+        )
+
+    def reduce(stage, position):
+        index = (1 << stage) - 1 + position
+        return pltpu.make_async_remote_copy(
+            src_ref=parts.at[place(position + (1 << stage), devices)],
+            dst_ref=landed.at[index],
+            send_sem=reduce_send.at[index],
+            recv_sem=reduce_recv.at[index],
+            device_id={"ep": partners[stage]},
+            device_id_type=pl.DeviceIdType.MESH,
+        )
+
+    def add(stage, position):
+        reduce(stage, position).wait_recv()
+        spot = place(position, devices)
+        total = parts[spot].astype(jnp.float32) + landed[(1 << stage) - 1 + position].astype(
+            jnp.float32
+        )
+        parts[spot] = total.astype(jnp.bfloat16)
+
+    def project(half):
+        first = half * (devices // 2)
+        block = (devices // 2) * count
+        step = 1024
+        gates = jnp.zeros((block, gate.shape[1]), jnp.float32)
+        ups = jnp.zeros((block, gate.shape[1]), jnp.float32)
+        for start in range(0, width, step):
+            part = rows[first : first + devices // 2, :, start : start + step].reshape(block, step)
+            gates += jnp.dot(
+                part, gate[start : start + step, :], preferred_element_type=jnp.float32
+            )
+            ups += jnp.dot(part, up[start : start + step, :], preferred_element_type=jnp.float32)
+        hidden[half * block : (half + 1) * block, :] = (
+            gates / (1.0 + jnp.exp(-gates)) * ups
+        ).astype(jnp.bfloat16)
+
+    def finish(position):
+        first = place(position, devices)
+        block = quarter * count
+        table = rows[first : first + quarter, :, width:].reshape(block, -1).astype(jnp.float32)
+        lanes = lax.broadcasted_iota(jnp.int32, table.shape, 1)
+        scale = jnp.sum(jnp.where(lanes == me // 2, table, 0.0), axis=1, keepdims=True)
+        units = hidden[first * count : (first + quarter) * count, :]
+        step = 512
+        for start in range(0, width, step):
+            product = jnp.dot(
+                units, down[:, start : start + step], preferred_element_type=jnp.float32
+            )
+            parts[first : first + quarter, :, start : start + step] = (
+                (product * scale).astype(jnp.bfloat16).reshape(quarter, count, step)
+            )
+
+    top = stages - 1
+    for stage in range(stages):
+        gather(stage, 0).start()
+    for stage in range(top - 1):
+        for position in range(1 << stage):
+            gather(stage, position).wait_recv()
+            for later in range(stage + 1, stages):
+                gather(later, position + (1 << stage)).start()
+    for position in range(quarter):
+        gather(top, position).wait_recv()
+    for load in loads:
+        load.wait()
+    project(0)
+    for position in range(quarter):
+        gather(top - 1, position).wait_recv()
+        gather(top, position + quarter).start()
+    for position in range(quarter, 2 * quarter):
+        gather(top, position).wait_recv()
+    project(1)
+
+    finish(3 * quarter)
+    for position in range(2 * quarter - 1, quarter - 1, -1):
+        reduce(top, position).start()
+    finish(2 * quarter)
+    for position in range(quarter - 1, -1, -1):
+        reduce(top, position).start()
+    finish(quarter)
+    for position in range(quarter - 1, -1, -1):
+        add(top, position + quarter)
+        reduce(top - 1, position).start()
+    finish(0)
+    for position in range(quarter - 1, -1, -1):
+        add(top, position)
+    for stage in range(top - 1, 0, -1):
+        upper = 1 << (stage - 1)
+        for position in range(upper - 1, -1, -1):
+            add(stage, position + upper)
+            reduce(stage - 1, position).start()
+        for position in range(upper - 1, -1, -1):
+            add(stage, position)
+    reduce(0, 0).wait_recv()
+    out_ref[...] = parts[0].astype(jnp.float32) + landed[0].astype(jnp.float32)
+    for stage in range(stages):
+        for position in range(1 << stage):
+            gather(stage, position).wait_send()
+            reduce(stage, position).wait_send()
+
+
+def exchange(packed, gate_weight, up_weight, down_weight, devices):
+    count, lanes = packed.shape
+    _, width, half = gate_weight.shape
+    dma = pltpu.SemaphoreType.DMA
+    return pl.pallas_call(
+        functools.partial(exchange_kernel, devices),
+        out_shape=jax.ShapeDtypeStruct((count, width), jnp.float32),
+        in_specs=[pl.BlockSpec(memory_space=pltpu.VMEM)] + [pl.BlockSpec(memory_space=pl.ANY)] * 3,
+        out_specs=pl.BlockSpec(memory_space=pltpu.VMEM),
+        scratch_shapes=[
+            pltpu.VMEM((devices, count, lanes), jnp.bfloat16),
+            pltpu.VMEM((devices, count, width), jnp.bfloat16),
+            pltpu.VMEM((devices - 1, count, width), jnp.bfloat16),
+            pltpu.VMEM((devices * count, half), jnp.bfloat16),
+            pltpu.VMEM((width, half), jnp.bfloat16),
+            pltpu.VMEM((width, half), jnp.bfloat16),
+            pltpu.VMEM((half, width), jnp.bfloat16),
+            dma((3,)),
+            dma((devices - 1,)),
+            dma((devices - 1,)),
+            dma((devices - 1,)),
+            dma((devices - 1,)),
+        ],
+        compiler_params=pltpu.CompilerParams(
+            collective_id=0, has_side_effects=True, vmem_limit_bytes=VMEM_BUDGET
+        ),
+    )(packed, gate_weight, up_weight, down_weight)
 
 
 def attention_rows(query_rows, key_rows, value_rows, length_rows):
@@ -56,6 +232,10 @@
         jnp.where(hits, route_weights.astype(jnp.float32)[:, :, None], 0.0), axis=1
     ).astype(jnp.bfloat16)
     packed = jnp.concatenate([normed, dense], axis=1)
+    held = 3 * devices * packed.size * 2 + 3 * gate_weight.size * 2
+    if held <= VMEM_BUDGET * 3 // 4 and devices >= 8 and devices & (devices - 1) == 0:
+        combined = exchange(packed, gate_weight, up_weight, down_weight, devices)
+        return (middle + combined).astype(jnp.bfloat16)
     gathered = lax.all_gather(packed, "ep", axis=0, tiled=True)
     rows = gathered[:, :width]
     scale = jnp.sum(

time: 252 us -> 81.4 us (0.32)
  waiting for transfers between devices: 205 us -> 0 us
  Pallas kernels: 0 us -> 68.4 us
  matrix products: 21.2 us -> 3.32 us
  between operations: 13.4 us -> 0.1 us
  other arithmetic: 7.12 us -> 2.39 us
    reduce_scatter x1 -> x0, waiting for transfers between devices: 139 us -> none  [local(): lax.psum_scatter(partial_out, 'ep', scatter_dimension=0, tiled=True)]
    pallas_call x0 -> x1, Pallas kernels: none -> 68.4 us  [exchange(): pl.pallas_call(functools.partial(exchange_kernel, devices), out_shape=jax...]
    all_gather x1 -> x0, waiting for transfers between devices: 65.3 us -> none  [local(): gathered = lax.all_gather(packed, 'ep', axis=0, tiled=True)]
    dot_general x2 -> x0, matrix products: 16.2 us -> none  [the longest x1 9.78 us: local(): jnp.dot(hidden, down_weight[0], preferred_element_type=jnp.float32)]
    unnamed x8 -> x18, local copies, waits for them, and re-layouts: 3.17 us -> 6.81 us
  transfers between devices with their start and end apart: 2 -> 0, of which waited for: 2 -> 0; matrix products, arithmetic and copies ran while one was open for 0% -> 0% of each run, Pallas kernels for 0% -> 0%
where the time goes in v2:
time: 81.4 us; the launch traced here: 81.1 us
  Pallas kernels  68.4 us (84%)
  local copies, waits for them, and re-layouts  6.88 us (8%)
  matrix products  3.32 us (4%)
  other arithmetic  2.39 us (3%)
    pallas_call x1, Pallas kernels, exchange(): pl.pallas_call(functools.partial(exchange_kernel, devices), out_shape=jax...  68.4 us
    unnamed x18, local copies, waits for them, and re-layouts  6.81 us
    dot_general x1, matrix products, attention_rows(): jnp.einsum('rgqc,rcgd->rgqd', weights, value_heads, preferred_element_typ...  2.41 us

profile of v2, /device:TPU:0, one launch (start us, length us, event | category | flops | bytes accessed | tf_op | source)
XLA Modules:
  0.0 81.1 jit_solution(11264735604791188237)
XLA Ops:
  0.0 0.0 copy-start
  0.0 1.0 %copy.22 = bf16[2,8,32,128]{3,2,1,0:T(8,128)(2,1)S(1)} copy(bf16[2,8,32,128]{3,1,2,0:T(8,128)(2,1)} %bitcast.42) | data formatting | bytes 262144
  1.0 0.7 iota_compare_fusion.1
  1.8 0.0 copy-done
  1.8 0.9 %fusion.12 = f32[16,2,16,192]{3,2,1,0:T(8,128)S(1)} fusion(bf16[16,2,16,128]{3,2,1,0:T(8,128)(2,1)S(1)} %bitcast.41, pred[16,192]{1,0:T(8,128)(4,1)S(1)} %iota_compare_fusion.1, bf16[16,192,256]{2,1,0:T(8,128)(2,1)S(1)} %copy-done), kind=kOutput, calls=%fused_computation.10 | convolution fusion | flops 25362432 | bytes 2100224 | tf_op jit(solution)/shard_map/rgqd,rcgd->rgqc/dot_general | solution.py:192
  2.7 0.3 fusion.23
  3.0 0.0 copy-start.4
  3.0 0.0 copy-start.5
  3.0 0.0 copy-start.6
  3.0 0.0 copy-start.7
  3.0 2.4 %fusion.18 = f32[16,2,16,128]{3,2,1,0:T(8,128)S(1)} fusion(f32[16,2,16]{2,1,0:T(2,128)S(1)} %fusion.23, f32[16,2,16,192]{3,2,1,0:T(8,128)S(1)} %fusion.12, bf16[16,192,256]{2,1,0:T(8,128)(2,1)} %param.13), kind=kOutput, calls=%fused_computation.12 | convolution fusion | flops 25592512 | bytes 2230272 | tf_op jit(solution)/shard_map/rgqc,rcgd->rgqd/dot_general | solution.py:200
  5.4 0.0 copy-done.4
  5.4 0.3 multiply_reduce_fusion
  5.7 0.0 copy-done.5
  5.7 0.2 multiply_convert_fusion
  5.9 0.0 copy-done.6
  5.9 0.1 copy.18
  6.0 0.0 copy-done.7
  6.0 0.1 copy.19
  6.1 0.1 select_reduce_fusion
  6.2 0.0 copy-start.1
  6.2 1.9 %copy-done.1 = bf16[1,4096,384]{2,1,0:T(8,128)(2,1)S(1)} copy-done((bf16[1,4096,384]{2,1,0:T(8,128)(2,1)S(1)}, bf16[1,4096,384]{2,1,0:T(8,128)(2,1)}, u32[]{:S(2)}) %copy-start.1) | copy-done | bytes 3145752
  8.1 0.0 copy-start.2
  8.1 1.9 %copy-done.2 = bf16[1,4096,384]{2,1,0:T(8,128)(2,1)S(1)} copy-done((bf16[1,4096,384]{2,1,0:T(8,128)(2,1)S(1)}, bf16[1,4096,384]{2,1,0:T(8,128)(2,1)}, u32[]{:S(2)}) %copy-start.2) | copy-done | bytes 3145752
  10.0 0.0 copy-start.3
  10.0 1.9 %copy-done.3 = bf16[1,384,4096]{2,1,0:T(8,128)(2,1)S(1)} copy-done((bf16[1,384,4096]{2,1,0:T(8,128)(2,1)S(1)}, bf16[1,384,4096]{2,1,0:T(8,128)(2,1)}, u32[]{:S(2)}) %copy-start.3) | copy-done | bytes 3145752
  11.9 68.4 %shard_map.109 = f32[16,4096]{1,0:T(8,128)S(1)} custom-call(bf16[16,4224]{1,0:T(8,128)(2,1)S(1)} %pad_maximum_fusion.own_ref, bf16[1,4096,384]{2,1,0:T(8,128)(2,1)S(1)} %copy-done.1, bf16[1,4096,384]{2,1,0:T(8,128)(2,1)S(1)} %copy-done.2, bf16[1,384,4096]{2,1,0:T(8,128)(2,1)S(1)} %copy-done.3), custom_call_target="tpu_custom_call" | custom-call | tf_op jit(solution)/shard_map/pallas_call | solution.py:160
  80.3 0.8 %add_convert_fusion = bf16[16,4096]{1,0:T(8,128)(2,1)} fusion(f32[16,4096]{1,0:T(8,128)S(1)} %shard_map.109, f32[2,8,32,128]{3,2,1,0:T(8,128)S(1)} %bitcast.40, bf16[16,4096]{1,0:T(8,128)(2,1)S(1)} %copy-done.4), kind=kLoop, calls=%fused_computation.15 | loop fusion | flops 262144 | bytes 786432 | tf_op jit(solution)/shard_map/convert_element_type | solution.py:238
  (3 shorter events, 0.0 us)
Async XLA Ops:
  0.0 1.8 %copy-start = (bf16[16,192,256]{2,1,0:T(8,128)(2,1)S(1)}, bf16[16,192,256]{2,1,0:T(8,128)(2,1)}, u32[]{:S(2)}) copy-start(bf16[16,192,256]{2,1,0:T(8,128)(2,1)} %param.12) | copy-start | bytes 4718596
  3.0 2.5 %copy-start.4 = (bf16[16,4096]{1,0:T(8,128)(2,1)S(1)}, bf16[16,4096]{1,0:T(8,128)(2,1)}, u32[]{:S(2)}) copy-start(bf16[16,4096]{1,0:T(8,128)(2,1)} %param.15) | copy-start | bytes 393220
  3.0 2.7 %copy-start.5 = (bf16[4096]{0:T(1024)(128)(2,1)S(1)}, bf16[4096]{0:T(1024)(128)(2,1)}, u32[]{:S(2)}) copy-start(bf16[4096]{0:T(1024)(128)(2,1)} %param.16) | copy-start | bytes 24580
  3.0 2.9 %copy-start.6 = (s32[16,8]{0,1:T(8,128)S(1)}, s32[16,8]{0,1:T(8,128)}, u32[]{:S(2)}) copy-start(s32[16,8]{0,1:T(8,128)} %param.17) | copy-start | bytes 1540
  3.0 3.0 %copy-start.7 = (bf16[16,8]{0,1:T(8,128)(2,1)S(1)}, bf16[16,8]{0,1:T(8,128)(2,1)}, u32[]{:S(2)}) copy-start(bf16[16,8]{0,1:T(8,128)(2,1)} %param.18) | copy-start | bytes 772
  6.2 1.9 %copy-start.1 = (bf16[1,4096,384]{2,1,0:T(8,128)(2,1)S(1)}, bf16[1,4096,384]{2,1,0:T(8,128)(2,1)}, u32[]{:S(2)}) copy-start(bf16[1,4096,384]{2,1,0:T(8,128)(2,1)} %gate_hbm.1) | copy-start | bytes 9437188
  8.1 1.9 %copy-start.2 = (bf16[1,4096,384]{2,1,0:T(8,128)(2,1)S(1)}, bf16[1,4096,384]{2,1,0:T(8,128)(2,1)}, u32[]{:S(2)}) copy-start(bf16[1,4096,384]{2,1,0:T(8,128)(2,1)} %up_hbm.1) | copy-start | bytes 9437188
  10.0 1.9 %copy-start.3 = (bf16[1,384,4096]{2,1,0:T(8,128)(2,1)S(1)}, bf16[1,384,4096]{2,1,0:T(8,128)(2,1)}, u32[]{:S(2)}) copy-start(bf16[1,384,4096]{2,1,0:T(8,128)(2,1)} %down_hbm.1) | copy-start | bytes 9437188

commit v3 on v2

--- a/solution.py
+++ b/solution.py
@@ -8,7 +8,7 @@
 from jax.sharding import PartitionSpec as P
 
 KVH = 2
-VMEM_BUDGET = 40 << 20
+VMEM_BUDGET = 62 << 20
 
 
 def place(position, devices):
@@ -16,13 +16,20 @@
     return (0, 2, 1, 3)[quarter] * (devices // 4) + rest
 
 
+def swapped(position, devices):
+    high, low = devices // 4, devices // 8
+    first, second = position // high % 2, position // low % 2
+    return position + (second - first) * (high - low)
+
+
 def exchange_kernel(
     devices, own_ref, gate_hbm, up_hbm, down_hbm, out_ref,
-    rows, parts, landed, hidden, gate, up, down,
+    rows, parts, landed, hidden, first_weights, down,
     load_sem, gather_send, gather_recv, reduce_send, reduce_recv,
 ):
     stages = devices.bit_length() - 1
     count, width = own_ref.shape[0], gate_hbm.shape[1]
+    half_units = gate_hbm.shape[2]
     quarter = devices // 4
     me = lax.axis_index("ep")
     core = me % 2
@@ -31,7 +38,7 @@
 
     loads = [
         pltpu.make_async_copy(source.at[0], target, load_sem.at[i])
-        for i, (source, target) in enumerate(((gate_hbm, gate), (up_hbm, up), (down_hbm, down)))
+        for i, (source, target) in enumerate(((gate_hbm, first_weights.at[:, :half_units]), (up_hbm, first_weights.at[:, half_units:]), (down_hbm, down)))
     ]
     for load in loads:
         load.start()
@@ -54,37 +61,40 @@
             device_id_type=pl.DeviceIdType.MESH,
         )
 
+    back = partners[:-3] + [partners[-2], partners[-3], partners[-1]]
+
+    def spot(position):
+        return place(swapped(position, devices), devices)
+
     def reduce(stage, position):
         index = (1 << stage) - 1 + position
         return pltpu.make_async_remote_copy(
-            src_ref=parts.at[place(position + (1 << stage), devices)],
+            src_ref=parts.at[spot(position + (1 << stage))],
             dst_ref=landed.at[index],
             send_sem=reduce_send.at[index],
             recv_sem=reduce_recv.at[index],
-            device_id={"ep": partners[stage]},
+            device_id={"ep": back[stage]},
             device_id_type=pl.DeviceIdType.MESH,
         )
 
     def add(stage, position):
         reduce(stage, position).wait_recv()
-        spot = place(position, devices)
-        total = parts[spot].astype(jnp.float32) + landed[(1 << stage) - 1 + position].astype(
-            jnp.float32
-        )
-        parts[spot] = total.astype(jnp.bfloat16)
+        total = parts[spot(position)].astype(jnp.float32) + landed[
+            (1 << stage) - 1 + position
+        ].astype(jnp.float32)
+        parts[spot(position)] = total.astype(jnp.bfloat16)
 
     def project(half):
         first = half * (devices // 2)
         block = (devices // 2) * count
         step = 1024
-        gates = jnp.zeros((block, gate.shape[1]), jnp.float32)
-        ups = jnp.zeros((block, gate.shape[1]), jnp.float32)
+        both = jnp.zeros((block, 2 * half_units), jnp.float32)
         for start in range(0, width, step):
             part = rows[first : first + devices // 2, :, start : start + step].reshape(block, step)
-            gates += jnp.dot(
-                part, gate[start : start + step, :], preferred_element_type=jnp.float32
+            both += jnp.dot(
+                part, first_weights[start : start + step, :], preferred_element_type=jnp.float32
             )
-            ups += jnp.dot(part, up[start : start + step, :], preferred_element_type=jnp.float32)
+        gates, ups = both[:, :half_units], both[:, half_units:]
         hidden[half * block : (half + 1) * block, :] = (
             gates / (1.0 + jnp.exp(-gates)) * ups
         ).astype(jnp.bfloat16)
@@ -117,26 +127,34 @@
         gather(top, position).wait_recv()
     for load in loads:
         load.wait()
+    eighth = quarter // 2
+    early = [*range(quarter + eighth - 1, quarter - 1, -1), *range(eighth - 1, -1, -1)]
+    late = [position + eighth for position in early]
     project(0)
-    for position in range(quarter):
+    finish(2 * quarter)
+    for position in early:
+        reduce(top, position).start()
+    for position in range(eighth):
         gather(top - 1, position).wait_recv()
         gather(top, position + quarter).start()
+    finish(0)
+    for position in range(eighth, quarter):
+        gather(top - 1, position).wait_recv()
+        gather(top, position + quarter).start()
+    for position in early[:eighth]:
+        add(top, position)
+        reduce(top - 1, position - quarter).start()
     for position in range(quarter, 2 * quarter):
         gather(top, position).wait_recv()
     project(1)
-
     finish(3 * quarter)
-    for position in range(2 * quarter - 1, quarter - 1, -1):
-        reduce(top, position).start()
-    finish(2 * quarter)
-    for position in range(quarter - 1, -1, -1):
+    for position in late:
         reduce(top, position).start()
     finish(quarter)
-    for position in range(quarter - 1, -1, -1):
-        add(top, position + quarter)
-        reduce(top - 1, position).start()
-    finish(0)
-    for position in range(quarter - 1, -1, -1):
+    for position in late[:eighth]:
+        add(top, position)
+        reduce(top - 1, position - quarter).start()
+    for position in late[eighth:] + early[eighth:]:
         add(top, position)
     for stage in range(top - 1, 0, -1):
         upper = 1 << (stage - 1)
@@ -160,15 +178,14 @@
     return pl.pallas_call(
         functools.partial(exchange_kernel, devices),
         out_shape=jax.ShapeDtypeStruct((count, width), jnp.float32),
-        in_specs=[pl.BlockSpec(memory_space=pltpu.VMEM)] + [pl.BlockSpec(memory_space=pl.ANY)] * 3,
+        in_specs=[pl.BlockSpec(memory_space=pltpu.VMEM)] + [pl.BlockSpec(memory_space=pltpu.HBM)] * 3,
         out_specs=pl.BlockSpec(memory_space=pltpu.VMEM),
         scratch_shapes=[
             pltpu.VMEM((devices, count, lanes), jnp.bfloat16),
             pltpu.VMEM((devices, count, width), jnp.bfloat16),
             pltpu.VMEM((devices - 1, count, width), jnp.bfloat16),
             pltpu.VMEM((devices * count, half), jnp.bfloat16),
-            pltpu.VMEM((width, half), jnp.bfloat16),
-            pltpu.VMEM((width, half), jnp.bfloat16),
+            pltpu.VMEM((width, 2 * half), jnp.bfloat16),
             pltpu.VMEM((half, width), jnp.bfloat16),
             dma((3,)),
             dma((devices - 1,)),

time: 81.4 us -> 71.2 us (0.87)
  Pallas kernels: 68.4 us -> 62.3 us
  local copies, waits for them, and re-layouts: 6.88 us -> 1.22 us
  other arithmetic: 2.39 us -> 4.01 us
    pallas_call x1, Pallas kernels: 68.4 us -> 62.3 us  [exchange(): pl.pallas_call(functools.partial(exchange_kernel, devices), out_shape=jax...]
    unnamed x18 -> x12, local copies, waits for them, and re-layouts: 6.81 us -> 1.14 us
    convert_element_type x1, other arithmetic: 0.82 us -> 1.77 us  [local(): return (middle + combined).astype(jnp.bfloat16)]
where the time goes in v3:
time: 71.2 us; the launch traced here: 71 us
  Pallas kernels  62.3 us (88%)
  other arithmetic  4.01 us (6%)
  matrix products  3.32 us (5%)
  local copies, waits for them, and re-layouts  1.22 us (2%)
    pallas_call x1, Pallas kernels, exchange(): pl.pallas_call(functools.partial(exchange_kernel, devices), out_shape=jax...  62.3 us
    dot_general x1, matrix products, attention_rows(): jnp.einsum('rgqc,rcgd->rgqd', weights, value_heads, preferred_element_typ...  2.41 us
    convert_element_type x1, other arithmetic, local(): return (middle + combined).astype(jnp.bfloat16)  1.77 us

profile of v3, /device:TPU:0, one launch (start us, length us, event | category | flops | bytes accessed | tf_op | source)
XLA Modules:
  0.0 71.0 jit_solution(13124101612089485051)
XLA Ops:
  0.0 0.0 copy-start
  0.0 1.0 %copy.22 = bf16[2,8,32,128]{3,2,1,0:T(8,128)(2,1)S(1)} copy(bf16[2,8,32,128]{3,1,2,0:T(8,128)(2,1)} %bitcast.42) | data formatting | bytes 262144
  1.0 0.7 %iota_compare_fusion.1 = pred[16,192]{1,0:T(8,128)(4,1)S(1)} fusion(s32[16]{0:T(128)} %param.14), kind=kLoop, calls=%fused_computation.22 | loop fusion | flops 3072 | bytes 3136 | tf_op jit(solution)/shard_map/lt | solution.py:212
  1.8 0.0 copy-done
  1.8 0.9 %fusion.12 = f32[16,2,16,192]{3,2,1,0:T(8,128)S(1)} fusion(bf16[16,2,16,128]{3,2,1,0:T(8,128)(2,1)S(1)} %bitcast.41, pred[16,192]{1,0:T(8,128)(4,1)S(1)} %iota_compare_fusion.1, bf16[16,192,256]{2,1,0:T(8,128)(2,1)S(1)} %copy-done), kind=kOutput, calls=%fused_computation.10 | convolution fusion | flops 25362432 | bytes 2100224 | tf_op jit(solution)/shard_map/rgqd,rcgd->rgqc/dot_general | solution.py:209
  2.7 0.3 fusion.23
  3.0 0.0 copy-start.1
  3.0 0.0 copy-start.2
  3.0 0.0 copy-start.3
  3.0 0.0 copy-start.4
  3.0 2.4 %fusion.18 = f32[16,2,16,128]{3,2,1,0:T(8,128)S(1)} fusion(f32[16,2,16]{2,1,0:T(2,128)S(1)} %fusion.23, f32[16,2,16,192]{3,2,1,0:T(8,128)S(1)} %fusion.12, bf16[16,192,256]{2,1,0:T(8,128)(2,1)} %param.13), kind=kOutput, calls=%fused_computation.12 | convolution fusion | flops 25592512 | bytes 2230272 | tf_op jit(solution)/shard_map/rgqc,rcgd->rgqd/dot_general | solution.py:217
  5.4 0.0 copy-done.1
  5.4 0.3 multiply_reduce_fusion
  5.7 0.0 copy-done.2
  5.7 0.2 multiply_convert_fusion
  5.9 0.0 copy-done.3
  5.9 0.1 copy.18
  6.0 0.0 copy-done.4
  6.0 0.1 copy.19
  6.1 0.1 select_reduce_fusion
  6.2 0.7 pad_maximum_fusion.own_ref
  6.9 62.3 %shard_map.109 = f32[16,4096]{1,0:T(8,128)} custom-call(bf16[16,4224]{1,0:T(8,128)(2,1)} %pad_maximum_fusion.own_ref, bf16[1,4096,384]{2,1,0:T(8,128)(2,1)} %gate_hbm.1, bf16[1,4096,384]{2,1,0:T(8,128)(2,1)} %up_hbm.1, bf16[1,384,4096]{2,1,0:T(8,128)(2,1)} %down_hbm.1), custom_call_target="tpu_custom_call" | custom-call | tf_op jit(solution)/shard_map/pallas_call | solution.py:178
  69.2 1.8 %add_convert_fusion = bf16[16,4096]{1,0:T(8,128)(2,1)} fusion(f32[16,4096]{1,0:T(8,128)} %shard_map.109, f32[2,8,32,128]{3,2,1,0:T(8,128)S(1)} %bitcast.40, bf16[16,4096]{1,0:T(8,128)(2,1)S(1)} %copy-done.1), kind=kLoop, calls=%fused_computation.15 | loop fusion | flops 262144 | bytes 786432 | tf_op jit(solution)/shard_map/convert_element_type | solution.py:255
  (2 shorter events, 0.0 us)
Async XLA Ops:
  0.0 1.8 %copy-start = (bf16[16,192,256]{2,1,0:T(8,128)(2,1)S(1)}, bf16[16,192,256]{2,1,0:T(8,128)(2,1)}, u32[]{:S(2)}) copy-start(bf16[16,192,256]{2,1,0:T(8,128)(2,1)} %param.12) | copy-start | bytes 4718596
  3.0 2.5 %copy-start.1 = (bf16[16,4096]{1,0:T(8,128)(2,1)S(1)}, bf16[16,4096]{1,0:T(8,128)(2,1)}, u32[]{:S(2)}) copy-start(bf16[16,4096]{1,0:T(8,128)(2,1)} %param.15) | copy-start | bytes 393220
  3.0 2.7 %copy-start.2 = (bf16[4096]{0:T(1024)(128)(2,1)S(1)}, bf16[4096]{0:T(1024)(128)(2,1)}, u32[]{:S(2)}) copy-start(bf16[4096]{0:T(1024)(128)(2,1)} %param.16) | copy-start | bytes 24580
  3.0 2.9 %copy-start.3 = (s32[16,8]{0,1:T(8,128)S(1)}, s32[16,8]{0,1:T(8,128)}, u32[]{:S(2)}) copy-start(s32[16,8]{0,1:T(8,128)} %param.17) | copy-start | bytes 1540
  3.0 3.0 %copy-start.4 = (bf16[16,8]{0,1:T(8,128)(2,1)S(1)}, bf16[16,8]{0,1:T(8,128)(2,1)}, u32[]{:S(2)}) copy-start(bf16[16,8]{0,1:T(8,128)(2,1)} %param.18) | copy-start | bytes 772

commit v4 on v3

--- a/solution.py
+++ b/solution.py
@@ -84,18 +84,17 @@
         ].astype(jnp.float32)
         parts[spot(position)] = total.astype(jnp.bfloat16)
 
-    def project(half):
-        first = half * (devices // 2)
-        block = (devices // 2) * count
+    def project(first, taken):
+        block = taken * count
         step = 1024
         both = jnp.zeros((block, 2 * half_units), jnp.float32)
         for start in range(0, width, step):
-            part = rows[first : first + devices // 2, :, start : start + step].reshape(block, step)
+            part = rows[first : first + taken, :, start : start + step].reshape(block, step)
             both += jnp.dot(
                 part, first_weights[start : start + step, :], preferred_element_type=jnp.float32
             )
         gates, ups = both[:, :half_units], both[:, half_units:]
-        hidden[half * block : (half + 1) * block, :] = (
+        hidden[first * count : first * count + block, :] = (
             gates / (1.0 + jnp.exp(-gates)) * ups
         ).astype(jnp.bfloat16)
 
@@ -123,14 +122,15 @@
             gather(stage, position).wait_recv()
             for later in range(stage + 1, stages):
                 gather(later, position + (1 << stage)).start()
-    for position in range(quarter):
-        gather(top, position).wait_recv()
     for load in loads:
         load.wait()
     eighth = quarter // 2
     early = [*range(quarter + eighth - 1, quarter - 1, -1), *range(eighth - 1, -1, -1)]
     late = [position + eighth for position in early]
-    project(0)
+    project(0, quarter)
+    for position in range(quarter):
+        gather(top, position).wait_recv()
+    project(quarter, quarter)
     finish(2 * quarter)
     for position in early:
         reduce(top, position).start()
@@ -144,17 +144,20 @@
     for position in early[:eighth]:
         add(top, position)
         reduce(top - 1, position - quarter).start()
+    for position in early[eighth:]:
+        add(top, position)
+    project(2 * quarter, quarter)
+    finish(quarter)
     for position in range(quarter, 2 * quarter):
         gather(top, position).wait_recv()
-    project(1)
+    project(3 * quarter, quarter)
     finish(3 * quarter)
     for position in late:
         reduce(top, position).start()
-    finish(quarter)
     for position in late[:eighth]:
         add(top, position)
         reduce(top - 1, position - quarter).start()
-    for position in late[eighth:] + early[eighth:]:
+    for position in late[eighth:]:
         add(top, position)
     for stage in range(top - 1, 0, -1):
         upper = 1 << (stage - 1)

time: 71.2 us -> 69.9 us (0.982)
  Pallas kernels: 62.3 us -> 61.1 us
    pallas_call x1, Pallas kernels: 62.3 us -> 61.1 us  [exchange(): pl.pallas_call(functools.partial(exchange_kernel, devices), out_shape=jax...]
where the time goes in v4:
time: 69.9 us; the launch traced here: 69.7 us
  Pallas kernels  61.1 us (87%)
  other arithmetic  4.01 us (6%)
  matrix products  3.32 us (5%)
  local copies, waits for them, and re-layouts  1.22 us (2%)
    pallas_call x1, Pallas kernels, exchange(): pl.pallas_call(functools.partial(exchange_kernel, devices), out_shape=jax...  61.1 us
    dot_general x1, matrix products, attention_rows(): jnp.einsum('rgqc,rcgd->rgqd', weights, value_heads, preferred_element_typ...  2.41 us
    convert_element_type x1, other arithmetic, local(): return (middle + combined).astype(jnp.bfloat16)  1.77 us

profile of v4, /device:TPU:0, one launch (start us, length us, event | category | flops | bytes accessed | tf_op | source)
XLA Modules:
  0.0 69.7 jit_solution(7921702522756867364)
XLA Ops:
  0.0 0.0 copy-start
  0.0 1.0 %copy.22 = bf16[2,8,32,128]{3,2,1,0:T(8,128)(2,1)S(1)} copy(bf16[2,8,32,128]{3,1,2,0:T(8,128)(2,1)} %bitcast.42) | data formatting | bytes 262144
  1.0 0.7 %iota_compare_fusion.1 = pred[16,192]{1,0:T(8,128)(4,1)S(1)} fusion(s32[16]{0:T(128)} %param.14), kind=kLoop, calls=%fused_computation.22 | loop fusion | flops 3072 | bytes 3136 | tf_op jit(solution)/shard_map/lt | solution.py:215
  1.8 0.0 copy-done
  1.8 0.9 %fusion.12 = f32[16,2,16,192]{3,2,1,0:T(8,128)S(1)} fusion(bf16[16,2,16,128]{3,2,1,0:T(8,128)(2,1)S(1)} %bitcast.41, pred[16,192]{1,0:T(8,128)(4,1)S(1)} %iota_compare_fusion.1, bf16[16,192,256]{2,1,0:T(8,128)(2,1)S(1)} %copy-done), kind=kOutput, calls=%fused_computation.10 | convolution fusion | flops 25362432 | bytes 2100224 | tf_op jit(solution)/shard_map/rgqd,rcgd->rgqc/dot_general | solution.py:212
  2.7 0.3 fusion.23
  3.0 0.0 copy-start.1
  3.0 0.0 copy-start.2
  3.0 0.0 copy-start.3
  3.0 0.0 copy-start.4
  3.0 2.4 %fusion.18 = f32[16,2,16,128]{3,2,1,0:T(8,128)S(1)} fusion(f32[16,2,16]{2,1,0:T(2,128)S(1)} %fusion.23, f32[16,2,16,192]{3,2,1,0:T(8,128)S(1)} %fusion.12, bf16[16,192,256]{2,1,0:T(8,128)(2,1)} %param.13), kind=kOutput, calls=%fused_computation.12 | convolution fusion | flops 25592512 | bytes 2230272 | tf_op jit(solution)/shard_map/rgqc,rcgd->rgqd/dot_general | solution.py:220
  5.4 0.0 copy-done.1
  5.4 0.3 multiply_reduce_fusion
  5.7 0.0 copy-done.2
  5.7 0.2 multiply_convert_fusion
  5.9 0.0 copy-done.3
  5.9 0.1 copy.18
  6.0 0.0 copy-done.4
  6.0 0.1 copy.19
  6.1 0.1 select_reduce_fusion
  6.2 0.7 pad_maximum_fusion.own_ref
  6.9 61.1 %shard_map.109 = f32[16,4096]{1,0:T(8,128)} custom-call(bf16[16,4224]{1,0:T(8,128)(2,1)} %pad_maximum_fusion.own_ref, bf16[1,4096,384]{2,1,0:T(8,128)(2,1)} %gate_hbm.1, bf16[1,4096,384]{2,1,0:T(8,128)(2,1)} %up_hbm.1, bf16[1,384,4096]{2,1,0:T(8,128)(2,1)} %down_hbm.1), custom_call_target="tpu_custom_call" | custom-call | tf_op jit(solution)/shard_map/pallas_call | solution.py:181
  67.9 1.8 %add_convert_fusion = bf16[16,4096]{1,0:T(8,128)(2,1)} fusion(f32[16,4096]{1,0:T(8,128)} %shard_map.109, f32[2,8,32,128]{3,2,1,0:T(8,128)S(1)} %bitcast.40, bf16[16,4096]{1,0:T(8,128)(2,1)S(1)} %copy-done.1), kind=kLoop, calls=%fused_computation.15 | loop fusion | flops 262144 | bytes 786432 | tf_op jit(solution)/shard_map/convert_element_type | solution.py:258
  (2 shorter events, 0.0 us)
Async XLA Ops:
  0.0 1.8 %copy-start = (bf16[16,192,256]{2,1,0:T(8,128)(2,1)S(1)}, bf16[16,192,256]{2,1,0:T(8,128)(2,1)}, u32[]{:S(2)}) copy-start(bf16[16,192,256]{2,1,0:T(8,128)(2,1)} %param.12) | copy-start | bytes 4718596
  3.0 2.5 %copy-start.1 = (bf16[16,4096]{1,0:T(8,128)(2,1)S(1)}, bf16[16,4096]{1,0:T(8,128)(2,1)}, u32[]{:S(2)}) copy-start(bf16[16,4096]{1,0:T(8,128)(2,1)} %param.15) | copy-start | bytes 393220
  3.0 2.7 %copy-start.2 = (bf16[4096]{0:T(1024)(128)(2,1)S(1)}, bf16[4096]{0:T(1024)(128)(2,1)}, u32[]{:S(2)}) copy-start(bf16[4096]{0:T(1024)(128)(2,1)} %param.16) | copy-start | bytes 24580
  3.0 2.9 %copy-start.3 = (s32[16,8]{0,1:T(8,128)S(1)}, s32[16,8]{0,1:T(8,128)}, u32[]{:S(2)}) copy-start(s32[16,8]{0,1:T(8,128)} %param.17) | copy-start | bytes 1540
  3.0 3.0 %copy-start.4 = (bf16[16,8]{0,1:T(8,128)(2,1)S(1)}, bf16[16,8]{0,1:T(8,128)(2,1)}, u32[]{:S(2)}) copy-start(bf16[16,8]{0,1:T(8,128)(2,1)} %param.18) | copy-start | bytes 772
